TPU v7x, 512 devices: a whole 4x8x8 slice. The times are simulated.
512 devices in a mesh: rep: 32 (over y, z_lo, core), fsdp: 16 (over z_hi, x).
Axes of the slice: x: 4, y: 8, z: 8 (z_hi: 4, z_lo: 2; z = z_hi * 2 + z_lo), core: 2. Of those that a mesh axis runs over, the one named last changes fastest.
Arguments:
- tokens: bfloat16 [16384, 4096], P('rep', 'fsdp'), may hold values from -6 to 6
- gate_weight: bfloat16 [4096, 7168], P('rep', 'fsdp'), may hold values from -0.09375 to 0.09375
- up_act: bfloat16 [16384, 7168], P('rep', 'fsdp'), may hold values from -6 to 6
- cotangent: bfloat16 [16384, 7168], P('rep', 'fsdp'), may hold values from -0.099609375 to 0.099609375
Outputs:
- grad_sum: bfloat16 [4096, 7168], P('rep', 'fsdp')
- curvature: float32 [7168], P('fsdp')
- spread: float32 [7168], P('fsdp')
All inputs are finite; a program needn't handle non-finite values.
Results may differ from a plain program's by a relative error of at most 0.024.
Values may be sent and summed in bfloat16 or wider, within the bound.
No kernel may reach another device: no remote copies, remote signals or barrier semaphores. Data moves between devices by JAX's collectives and lax.ppermute only.
A program may use at most 64 MiB of HBM per device.

v0:
```python
import jax
import jax.numpy as jnp
from jax import lax
from jax.sharding import Mesh
from jax.sharding import PartitionSpec as P

REP = ("rep_0", "rep_1", "rep_2")


def copy_for_each(value, axis):
    count = lax.axis_size(axis)
    return lax.all_to_all(
        jnp.broadcast_to(value[None], (count, *value.shape)), axis, 0, 0, tiled=True
    )


def in_order(blocks, dim):
    blocks = jnp.moveaxis(blocks, 0, dim)
    lengths = blocks.shape
    return blocks.reshape(*lengths[:dim], lengths[dim] * lengths[dim + 1], *lengths[dim + 2 :])


def gathered_by_axis(value, axes, dim):
    far, near = axes
    blocks = copy_for_each(copy_for_each(value, far), near)
    return in_order(blocks.swapaxes(0, 1).reshape(-1, *value.shape), dim)


def padded_to(lines, count):
    spare = -len(lines) % count
    return jnp.pad(lines, [(0, spare)] + [(0, 0)] * (lines.ndim - 1))


def in_blocks(value, dim, count):
    lengths = value.shape
    blocks = value.reshape(*lengths[:dim], count, lengths[dim] // count, *lengths[dim + 1 :])
    return jnp.moveaxis(blocks, dim, 0)


def summed_on_arrival(value, axis, dim):
    count = lax.axis_size(axis)
    blocks = lax.all_to_all(in_blocks(value, dim, count), axis, 0, 0, tiled=True)
    return jnp.sum(blocks.astype(jnp.float32), axis=0)


def sum_in_two_steps(value, axes, dim):
    far, near = axes
    own = summed_on_arrival(in_blocks(value, dim, lax.axis_size(far)), near, dim + 1)
    return jnp.sum(
        lax.all_to_all(own.astype(jnp.bfloat16), far, 0, 0, tiled=True).astype(jnp.float32), axis=0
    )


def total_of(value, axes):
    lines = value.reshape(-1, value.shape[-1])
    padded = padded_to(lines, lax.axis_size(axes[0]) * lax.axis_size(axes[1]))
    whole = gathered_by_axis(sum_in_two_steps(padded, axes, 0).astype(jnp.bfloat16), axes, 0)
    return lax.slice_in_dim(whole, 0, len(lines)).reshape(value.shape).astype(jnp.float32)


def over_copies(value, axis):
    everything = copy_for_each(value, axis)
    return jnp.sum(everything, axis=0)


def in_one(arrays, axis):
    ravelled, at, outs = (jnp.concatenate([a.reshape(-1) for a in arrays]), 0, [])
    running = over_copies(ravelled, axis)
    for a in arrays:
        outs.append(running[at : at + a.size].reshape(a.shape))
        at += a.size
    return tuple(outs)


def shards(tokens, gate_weight, up_act, cotangent):
    features_all = lax.all_gather(tokens, "fsdp", axis=1, tiled=True)
    replicas = lax.axis_size(REP)
    gate_pre = jnp.dot(
        features_all,
        gathered_by_axis(gate_weight, (("rep_0", "rep_1"), "rep_2"), 0),
        preferred_element_type=jnp.float32,
    )
    sigmoid_gate = jax.nn.sigmoid(gate_pre)
    deriv_one = sigmoid_gate * (1.0 + gate_pre * (1.0 - sigmoid_gate))
    deriv_two = sigmoid_gate * (1.0 - sigmoid_gate) * (2.0 + gate_pre * (1.0 - 2.0 * sigmoid_gate))
    weighted = cotangent.astype(jnp.float32) * up_act.astype(jnp.float32)
    token_coeff = (weighted * deriv_one).astype(jnp.bfloat16)
    bend_weight = weighted * deriv_two
    rep_grad = lax.dot_general(
        features_all, token_coeff, (((0,), (0,)), ((), ())), preferred_element_type=jnp.float32
    ).astype(jnp.bfloat16)
    own_proj = jnp.dot(features_all, rep_grad, preferred_element_type=jnp.float32)
    grad_full = total_of(
        rep_grad.astype(jnp.float32).astype(jnp.bfloat16), (("rep_0", "rep_1"), "rep_2")
    ).astype(jnp.bfloat16)
    shard_rows = grad_full.shape[0] // replicas
    grad_shard = lax.dynamic_slice_in_dim(
        grad_full, lax.axis_index(REP) * shard_rows, shard_rows, 0
    )
    mean_proj = jnp.dot(features_all, grad_full, preferred_element_type=jnp.float32) / replicas
    deviate = own_proj - mean_proj
    curv_part = jnp.sum(bend_weight * mean_proj * mean_proj, axis=0)
    spread_part = jnp.sum(bend_weight * deviate * deviate, axis=0)
    curvature, spread_total = in_one((curv_part, spread_part), REP)
    return (grad_shard, curvature, spread_total / (replicas - 1))


def solution(mesh):
    torus = Mesh(
        mesh.devices.reshape(8, 2, 2, mesh.shape["fsdp"]), ("rep_0", "rep_1", "rep_2", "fsdp")
    )
    in_specs = (P(REP, "fsdp"), P(REP, "fsdp"), P(REP, "fsdp"), P(REP, "fsdp"))
    out_specs = (P(REP, "fsdp"), P("fsdp"), P("fsdp"))
    return jax.shard_map(
        shards, mesh=torus, in_specs=in_specs, out_specs=out_specs, check_vma=False
    )
```

profile of v0, /device:TPU:1, one launch (start us, length us, event | category | flops | bytes accessed | tf_op | source)
XLA Modules:
  0.0 298.9 jit_solution(17605486827183492126)
XLA Ops:
  7.9 1.2 broadcast_in_dim.10
  9.2 53.8 %all_to_all.36 = bf16[16,128,448]{1,2,0:T(8,128)(2,1)S(1)} all-to-all(bf16[16,128,448]{1,2,0:T(8,128)(2,1)S(1)} %broadcast_in_dim.10), channel_id=1, replica_groups=mesh['rep_0'=8,'rep_1'=2,'rep_2'=2,'fsdp'=16] {'rep_0','rep_1'}, dimensions={0} | all-to-all | bytes 3670016 | tf_op jit(solution)/shard_map/all_to_all | solution.py:12
  63.0 1.2 copy.28
  64.6 8.7 %all_to_all.37 = bf16[2,16,128,448]{2,1,3,0:T(8,128)(2,1)S(1)} all-to-all(bf16[2,16,128,448]{2,1,3,0:T(8,128)(2,1)S(1)} %broadcast_in_dim.11), channel_id=1, replica_groups=mesh['rep_0'=8,'rep_1'=2,'rep_2'=2,'fsdp'=16] {'rep_2'}, dimensions={0} | all-to-all | bytes 7340032 | tf_op jit(solution)/shard_map/all_to_all | solution.py:12
  73.3 7.5 %copy.29 = bf16[16,2,128,448]{2,1,0,3:T(2,128)(2,1)} copy(bf16[16,2,128,448]{2,0,3,1:T(8,128)(2,1)S(1)} %bitcast.29) | data formatting | bytes 7340032 | tf_op jit(solution)/shard_map/transpose | solution.py:26
  80.8 7.2 %reshape_reshape.9 = bf16[4096,448]{0,1:T(8,128)(2,1)} reshape(bf16[16,2,128,448]{2,1,0,3:T(2,128)(2,1)} %copy.29) | data formatting | bytes 7340032 | tf_op jit(solution)/shard_map/reshape;reshape | solution.py:20
  88.0 24.2 %all-gather.2.cloned.1.call-done = bf16[512,4096]{1,0:T(8,128)(2,1)} async-done(((bf16[512,256]{1,0:T(8,128)(2,1)}), bf16[512,4096]{1,0:T(8,128)(2,1)}) %all-gather.2.cloned.1.call-update) | async-done | bytes 4194320 | tf_op jit(solution)/shard_map/all_gather | solution.py:76
  112.2 5.5 %fusion.13 = f32[512,448]{0,1:T(8,128)S(1)} fusion(bf16[512,4096]{1,0:T(8,128)(2,1)} %all-gather.2.cloned.1.call-done, bf16[4096,448]{0,1:T(8,128)(2,1)} %reshape_reshape.9), kind=kOutput, calls=%fused_computation.25 | convolution fusion | flops 1879048192 | bytes 8781824 | tf_op jit(solution)/shard_map/dot_general | solution.py:78
  117.8 4.1 %convolution_convert_fusion = bf16[448,4096]{1,0:T(8,128)(2,1)} fusion(bf16[512,4096]{1,0:T(8,128)(2,1)S(1)} %copy-done.1, f32[512,448]{0,1:T(8,128)S(1)} %fusion.13, bf16[512,448]{0,1:T(8,128)(2,1)S(1)} %copy-done.3, bf16[512,448]{0,1:T(8,128)(2,1)S(1)} %copy-done.4), kind=kOutput, calls=%fused_computation | convolution fusion | flops 1883635712 | bytes 9699328 | tf_op jit(solution)/shard_map/dot_general | solution.py:89
  121.9 7.1 %reshape_reshape.10 = bf16[16,2,128,448]{2,1,0,3:T(2,128)(2,1)} reshape(bf16[4096,448]{0,1:T(8,128)(2,1)} %bitcast.32) | data formatting | bytes 7340032 | tf_op jit(solution)/shard_map/reshape;reshape | solution.py:36
  129.0 2.5 copy.41
  131.5 7.9 %all_to_all.38 = bf16[2,16,128,448]{2,1,3,0:T(8,128)(2,1)} all-to-all(bf16[2,16,128,448]{2,1,3,0:T(8,128)(2,1)S(1)} %bitcast.30), channel_id=1, replica_groups=mesh['rep_0'=8,'rep_1'=2,'rep_2'=2,'fsdp'=16] {'rep_2'}, dimensions={0} | all-to-all | bytes 7340032 | tf_op jit(solution)/shard_map/all_to_all | solution.py:42
  139.5 4.0 %reduce_sum.51 = bf16[16,128,448]{1,0,2:T(8,128)(2,1)S(1)} reduce(bf16[2,16,128,448]{2,1,3,0:T(8,128)(2,1)} %all_to_all.38, bf16[]{:T(256)} %constant.11.clone.1), dimensions={0}, to_apply=%region_0.1 | reduce | flops 917504 | bytes 5505026 | tf_op jit(solution)/shard_map/reduce_sum | solution.py:43
  143.9 51.3 %all_to_all.39 = bf16[16,128,448]{1,2,0:T(8,128)(2,1)S(1)} all-to-all(bf16[16,128,448]{1,2,0:T(8,128)(2,1)S(1)} %copy.32), channel_id=1, replica_groups=mesh['rep_0'=8,'rep_1'=2,'rep_2'=2,'fsdp'=16] {'rep_0','rep_1'}, dimensions={0} | all-to-all | bytes 3670016 | tf_op jit(solution)/shard_map/all_to_all | solution.py:50
  195.8 47.7 %all_to_all.40 = bf16[16,128,448]{1,2,0:T(8,128)(2,1)S(1)} all-to-all(bf16[16,128,448]{1,2,0:T(8,128)(2,1)S(1)} %broadcast_in_dim.12), channel_id=1, replica_groups=mesh['rep_0'=8,'rep_1'=2,'rep_2'=2,'fsdp'=16] {'rep_0','rep_1'}, dimensions={0} | all-to-all | bytes 3670016 | tf_op jit(solution)/shard_map/all_to_all | solution.py:12
  243.5 1.2 copy.33
  245.2 8.8 %all_to_all.41 = bf16[2,16,128,448]{2,1,3,0:T(8,128)(2,1)S(1)} all-to-all(bf16[2,16,128,448]{2,1,3,0:T(8,128)(2,1)S(1)} %broadcast_in_dim.13), channel_id=1, replica_groups=mesh['rep_0'=8,'rep_1'=2,'rep_2'=2,'fsdp'=16] {'rep_2'}, dimensions={0} | all-to-all | bytes 7340032 | tf_op jit(solution)/shard_map/all_to_all | solution.py:12
  254.0 7.5 %copy.34 = bf16[16,2,128,448]{2,1,0,3:T(2,128)(2,1)} copy(bf16[16,2,128,448]{2,0,3,1:T(8,128)(2,1)S(1)} %bitcast.31) | data formatting | bytes 7340032 | tf_op jit(solution)/shard_map/transpose | solution.py:26
  261.5 7.2 %reshape_reshape.11 = bf16[4096,448]{0,1:T(8,128)(2,1)} reshape(bf16[16,2,128,448]{2,1,0,3:T(2,128)(2,1)} %copy.34) | data formatting | bytes 7340032 | tf_op jit(solution)/shard_map/reshape;reshape | solution.py:20
  268.8 6.0 %fusion.9 = (f32[448]{0:T(512)S(1)}, f32[512,448]{0,1:T(8,128)S(1)}) fusion(f32[512,448]{0,1:T(8,128)S(1)} %copy-done.6, bf16[512,448]{0,1:T(8,128)(2,1)S(1)} %copy-done.3, bf16[512,448]{0,1:T(8,128)(2,1)S(1)} %copy-done.4, bf16[4096,448]{0,1:T(8,128)(2,1)} %reshape_reshape.11, bf16[512,4096]{1,0:T(8,128)(2,1)} %all-gather.2.cloned.1.call-done), kind=kOutput, calls=%fused_computation.17 | convolution fusion | flops 1883176448 | bytes 10618624 | tf_op jit(solution)/shard_map/dot_general | solution.py:100
  274.8 2.6 fusion.2
  278.2 3.9 %all-to-all-start.6 = ((f32[32,1,896]{2,1,0:T(1,128)}), f32[32,1,896]{2,1,0:T(1,128)S(1)}, u32[]{:S(2)}, u32[]{:S(2)}) async-start(f32[32,1,896]{2,1,0:T(1,128)} %broadcast_in_dim.14), calls=%async_computation.6 | async-start | bytes 229376 | tf_op jit(solution)/shard_map/all_to_all | solution.py:12
  282.1 1.6 constant_dynamic-slice_fusion
  283.7 7.6 %all-to-all-done.6 = f32[32,1,896]{2,1,0:T(1,128)S(1)} async-done(((f32[32,1,896]{2,1,0:T(1,128)}), f32[32,1,896]{2,1,0:T(1,128)S(1)}, u32[]{:S(2)}, u32[]{:S(2)}) %all-to-all-start.6) | async-done | bytes 114720 | tf_op jit(solution)/shard_map/all_to_all | solution.py:12
  (25 shorter events, 4.3 us)
Async XLA Ops:
  7.2 105.0 %all-gather.2.cloned.1.call-start = ((), (), s32[]{:S(2)}) async-start(), calls=%async_computation.7 | async-start | bytes 4456448 | tf_op jit(solution)/shard_map/all_gather | solution.py:76
  88.0 29.8 %copy-start.3 = (bf16[512,448]{0,1:T(8,128)(2,1)S(1)}, bf16[512,448]{0,1:T(8,128)(2,1)}, u32[]{:S(2)}) copy-start(bf16[512,448]{0,1:T(8,128)(2,1)} %param.6) | copy-start | bytes 1376260
  88.0 29.8 %copy-start.4 = (bf16[512,448]{0,1:T(8,128)(2,1)S(1)}, bf16[512,448]{0,1:T(8,128)(2,1)}, u32[]{:S(2)}) copy-start(bf16[512,448]{0,1:T(8,128)(2,1)} %param.7) | copy-start | bytes 1376260
  112.2 5.6 %copy-start.1 = (bf16[512,4096]{1,0:T(8,128)(2,1)S(1)}, bf16[512,4096]{1,0:T(8,128)(2,1)}, u32[]{:S(2)}) copy-start(bf16[512,4096]{1,0:T(8,128)(2,1)} %all-gather.2.cloned.1.call-done) | copy-start | bytes 12582916
  117.8 4.1 %copy-start.5 = (f32[512,448]{0,1:T(8,128)}, f32[512,448]{0,1:T(8,128)S(1)}, u32[]{:S(2)}) copy-start(f32[512,448]{0,1:T(8,128)S(1)} %fusion.13) | copy-start | bytes 2752516
  261.5 7.2 %copy-start.6 = (f32[512,448]{0,1:T(8,128)S(1)}, f32[512,448]{0,1:T(8,128)}, u32[]{:S(2)}) copy-start(f32[512,448]{0,1:T(8,128)} %copy-done.5) | copy-start | bytes 2752516
  268.8 6.0 %copy-start = (bf16[448,4096]{1,0:T(8,128)(2,1)S(1)}, bf16[448,4096]{1,0:T(8,128)(2,1)}, u32[]{:S(2)}) copy-start(bf16[448,4096]{1,0:T(8,128)(2,1)} %convolution_convert_fusion) | copy-start | bytes 11010052
  268.8 6.1 %copy-start.2 = (bf16[512,4096]{1,0:T(8,128)(2,1)S(1)}, bf16[512,4096]{1,0:T(8,128)(2,1)}, u32[]{:S(2)}) copy-start(bf16[512,4096]{1,0:T(8,128)(2,1)} %all-gather.2.cloned.1.call-done) | copy-start | bytes 12582916
  278.2 13.1 %all-to-all-start.6 = ((f32[32,1,896]{2,1,0:T(1,128)}), f32[32,1,896]{2,1,0:T(1,128)S(1)}, u32[]{:S(2)}, u32[]{:S(2)}) async-start(f32[32,1,896]{2,1,0:T(1,128)} %broadcast_in_dim.14), calls=%async_computation.6 | async-start | bytes 229376 | tf_op jit(solution)/shard_map/all_to_all | solution.py:12
Sparse Core Ops, SparseCore 0:
  11.0 101.1 all-gather.1
where the time goes:
time: 300 us; the launch traced here: 299 us
  blocking collectives  178 us (59%)
  local copies, waits for them, and re-layouts  46.7 us (16%)
  waiting for transfers between devices  32.5 us (11%)
  matrix products  18.3 us (6%)
  between operations  14.2 us (5%)
  other arithmetic  5.04 us (2%)
  starting transfers between devices  3.92 us (1%)
    all_to_all x4, blocking collectives, copy_for_each(): lax.all_to_all(jnp.broadcast_to(value[None], (count, *value.shape)), axis...  119 us
    all_to_all x1, blocking collectives, sum_in_two_steps(): lax.all_to_all(own.astype(jnp.bfloat16), far, 0, 0, tiled=True)  51.3 us
    all_gather x1, waiting for transfers between devices, shards(): features_all = lax.all_gather(tokens, 'fsdp', axis=1, tiled=True)  24.2 us
    transpose x2, local copies, waits for them, and re-layouts, gathered_by_axis(): return in_order(blocks.swapaxes(0, 1).reshape(-1, *value.shape), dim)  15 us
    another operation x2, local copies, waits for them, and re-layouts, in_order(): blocks.reshape(*lengths[:dim], lengths[dim] * lengths[dim + 1], *lengths[...  14.4 us
    another operation x2, local copies, waits for them, and re-layouts, in_blocks(): value.reshape(*lengths[:dim], count, lengths[dim] // count, *lengths[dim...  9.59 us
    all_to_all x1, blocking collectives, summed_on_arrival(): lax.all_to_all(in_blocks(value, dim, count), axis, 0, 0, tiled=True)  7.95 us
    all_to_all x1, waiting for transfers between devices, copy_for_each(): lax.all_to_all(jnp.broadcast_to(value[None], (count, *value.shape)), axis...  7.6 us
  transfers between devices with their start and end apart: 2, of which 2 were waited for; matrix products, arithmetic and copies ran while one was open for 6% of the time, Pallas kernels for 0%

commit v1 on v0

--- a/solution.py
+++ b/solution.py
@@ -73,7 +73,8 @@
 
 
 def shards(tokens, gate_weight, up_act, cotangent):
-    features_all = lax.all_gather(tokens, "fsdp", axis=1, tiled=True)
+    sent = jnp.stack([tokens] * lax.axis_size("fsdp"))
+    features_all = jnp.concatenate(lax.all_to_all(sent, "fsdp", 0, 0), axis=1)
     replicas = lax.axis_size(REP)
     gate_pre = jnp.dot(
         features_all,

time: 300 us -> 367 us (1.22)
  waiting for transfers between devices: 32.5 us -> 132 us
  blocking collectives: 178 us -> 127 us
  starting transfers between devices: 3.92 us -> 25.2 us
  between operations: 14.2 us -> 0.78 us
  local copies, waits for them, and re-layouts: 46.7 us -> 52.5 us
  matrix products: 18.3 us -> 22.8 us
    all_to_all x0 -> x1, waiting for transfers between devices: none -> 83 us  [shards(): features_all = jnp.concatenate(lax.all_to_all(sent, 'fsdp', 0, 0), axis=1)]
    all_to_all x4 -> x3, blocking collectives: 119 us -> 68 us  [copy_for_each(): lax.all_to_all(jnp.broadcast_to(value[None], (count, *value.shape)), axis...]
    all_to_all x1 -> x2, waiting for transfers between devices: 7.6 us -> 49.4 us  [copy_for_each(): lax.all_to_all(jnp.broadcast_to(value[None], (count, *value.shape)), axis...]
    all_gather x1 -> x0, waiting for transfers between devices: 24.2 us -> none  [shards(): features_all = lax.all_gather(tokens, 'fsdp', axis=1, tiled=True)]
    all_to_all x0 -> x1, starting transfers between devices: none -> 11.8 us  [shards(): features_all = jnp.concatenate(lax.all_to_all(sent, 'fsdp', 0, 0), axis=1)]
    all_to_all x1 -> x2, starting transfers between devices: 3.88 us -> 13.4 us  [copy_for_each(): lax.all_to_all(jnp.broadcast_to(value[None], (count, *value.shape)), axis...]
  transfers between devices with their start and end apart: 2 -> 3, of which waited for: 2 -> 3; matrix products, arithmetic and copies ran while one was open for 6% -> 5% of each run, Pallas kernels for 0% -> 0%
where the time goes in v1:
time: 367 us; the launch traced here: 366 us
  waiting for transfers between devices  132 us (36%)
  blocking collectives  127 us (35%)
  local copies, waits for them, and re-layouts  52.5 us (14%)
  starting transfers between devices  25.2 us (7%)
  matrix products  22.8 us (6%)
  other arithmetic  5.04 us (1%)
    all_to_all x1, waiting for transfers between devices, shards(): features_all = jnp.concatenate(lax.all_to_all(sent, 'fsdp', 0, 0), axis=1)  83 us
    all_to_all x3, blocking collectives, copy_for_each(): lax.all_to_all(jnp.broadcast_to(value[None], (count, *value.shape)), axis...  68 us
    all_to_all x2, waiting for transfers between devices, copy_for_each(): lax.all_to_all(jnp.broadcast_to(value[None], (count, *value.shape)), axis...  49.4 us
    all_to_all x1, blocking collectives, sum_in_two_steps(): lax.all_to_all(own.astype(jnp.bfloat16), far, 0, 0, tiled=True)  49 us
    transpose x2, local copies, waits for them, and re-layouts, gathered_by_axis(): return in_order(blocks.swapaxes(0, 1).reshape(-1, *value.shape), dim)  17.1 us
    another operation x2, local copies, waits for them, and re-layouts, in_order(): blocks.reshape(*lengths[:dim], lengths[dim] * lengths[dim + 1], *lengths[...  14.4 us
    all_to_all x2, starting transfers between devices, copy_for_each(): lax.all_to_all(jnp.broadcast_to(value[None], (count, *value.shape)), axis...  13.4 us
    all_to_all x1, starting transfers between devices, shards(): features_all = jnp.concatenate(lax.all_to_all(sent, 'fsdp', 0, 0), axis=1)  11.8 us
  transfers between devices with their start and end apart: 3, of which 3 were waited for; matrix products, arithmetic and copies ran while one was open for 5% of the time, Pallas kernels for 0%

profile of v1, /device:TPU:1, one launch (start us, length us, event | category | flops | bytes accessed | tf_op | source)
XLA Modules:
  0.0 365.8 jit_solution(12062016937001300600)
XLA Ops:
  0.6 2.5 broadcast_in_dim.10
  3.2 9.6 %all-to-all-start.1 = ((bf16[16,128,448]{1,2,0:T(8,128)(2,1)}), bf16[16,128,448]{1,2,0:T(8,128)(2,1)S(1)}, u32[]{:S(2)}, u32[]{:S(2)}) async-start(bf16[16,128,448]{1,2,0:T(8,128)(2,1)} %broadcast_in_dim.10), calls=%async_computation.1 | async-start | bytes 3670016 | tf_op jit(solution)/shard_map/all_to_all | solution.py:12
  12.9 41.8 %all-to-all-done.1 = bf16[16,128,448]{1,2,0:T(8,128)(2,1)S(1)} async-done(((bf16[16,128,448]{1,2,0:T(8,128)(2,1)}), bf16[16,128,448]{1,2,0:T(8,128)(2,1)S(1)}, u32[]{:S(2)}, u32[]{:S(2)}) %all-to-all-start.1) | async-done | bytes 1835040 | tf_op jit(solution)/shard_map/all_to_all | solution.py:12
  56.4 11.5 %all_to_all.41 = bf16[2,16,128,448]{2,1,3,0:T(8,128)(2,1)} all-to-all(bf16[2,16,128,448]{2,1,3,0:T(8,128)(2,1)S(1)} %broadcast_in_dim.11), channel_id=1, replica_groups=mesh['rep_0'=8,'rep_1'=2,'rep_2'=2,'fsdp'=16] {'rep_2'}, dimensions={0} | all-to-all | bytes 7340032 | tf_op jit(solution)/shard_map/all_to_all | solution.py:12
  67.8 2.4 stack.2
  70.2 11.8 %all-to-all-start = ((bf16[16,512,256]{1,2,0:T(8,128)(2,1)}), bf16[16,512,256]{1,2,0:T(8,128)(2,1)}, u32[]{:S(2)}, u32[]{:S(2)}) async-start(bf16[16,512,256]{1,2,0:T(8,128)(2,1)} %stack.2), calls=%async_computation | async-start | bytes 8388608 | tf_op jit(solution)/shard_map/all_to_all | solution.py:77
  82.0 9.5 %copy.34 = bf16[16,2,128,448]{2,1,0,3:T(2,128)(2,1)} copy(bf16[16,2,128,448]{2,0,3,1:T(8,128)(2,1)} %bitcast.32) | data formatting | bytes 7340032 | tf_op jit(solution)/shard_map/transpose | solution.py:26
  91.5 7.1 %reshape_reshape.9 = bf16[4096,448]{0,1:T(8,128)(2,1)} reshape(bf16[16,2,128,448]{2,1,0,3:T(2,128)(2,1)} %copy.34) | data formatting | bytes 7340032 | tf_op jit(solution)/shard_map/reshape;reshape | solution.py:20
  98.6 83.0 %all-to-all-done = bf16[16,512,256]{1,2,0:T(8,128)(2,1)} async-done(((bf16[16,512,256]{1,2,0:T(8,128)(2,1)}), bf16[16,512,256]{1,2,0:T(8,128)(2,1)}, u32[]{:S(2)}, u32[]{:S(2)}) %all-to-all-start) | async-done | bytes 4194336 | tf_op jit(solution)/shard_map/all_to_all | solution.py:77
  181.6 5.4 %fusion.13 = f32[512,448]{0,1:T(8,128)S(1)} fusion(bf16[4096,448]{0,1:T(8,128)(2,1)} %reshape_reshape.9, bf16[512,4096]{0,1:T(8,128)(2,1)} %bitcast.1), kind=kOutput, calls=%fused_computation.25 | convolution fusion | flops 1879048192 | bytes 8781824 | tf_op jit(solution)/shard_map/dot_general | solution.py:79
  187.1 6.6 %convolution_convert_fusion = bf16[448,4096]{1,0:T(8,128)(2,1)} fusion(bf16[512,4096]{0,1:T(8,128)(2,1)} %bitcast.1, f32[512,448]{0,1:T(8,128)S(1)} %fusion.13, bf16[512,448]{0,1:T(8,128)(2,1)S(1)} %copy-done.2, bf16[512,448]{0,1:T(8,128)(2,1)S(1)} %copy-done.3), kind=kOutput, calls=%fused_computation | convolution fusion | flops 1883635712 | bytes 9699328 | tf_op jit(solution)/shard_map/dot_general | solution.py:90
  193.7 7.1 %reshape_reshape.10 = bf16[16,2,128,448]{2,1,0,3:T(2,128)(2,1)} reshape(bf16[4096,448]{0,1:T(8,128)(2,1)} %bitcast.35) | data formatting | bytes 7340032 | tf_op jit(solution)/shard_map/reshape;reshape | solution.py:36
  200.8 2.5 copy.46
  203.3 10.0 %all_to_all.42 = bf16[2,16,128,448]{2,1,3,0:T(8,128)(2,1)} all-to-all(bf16[2,16,128,448]{2,1,3,0:T(8,128)(2,1)S(1)} %bitcast.33), channel_id=1, replica_groups=mesh['rep_0'=8,'rep_1'=2,'rep_2'=2,'fsdp'=16] {'rep_2'}, dimensions={0} | all-to-all | bytes 7340032 | tf_op jit(solution)/shard_map/all_to_all | solution.py:42
  213.4 4.0 %reduce_sum.51 = bf16[16,128,448]{1,0,2:T(8,128)(2,1)S(1)} reduce(bf16[2,16,128,448]{2,1,3,0:T(8,128)(2,1)} %all_to_all.42, bf16[]{:T(256)} %constant.11.clone.1), dimensions={0}, to_apply=%region_0.1 | reduce | flops 917504 | bytes 5505026 | tf_op jit(solution)/shard_map/reduce_sum | solution.py:43
  217.8 49.0 %all_to_all.43 = bf16[16,128,448]{1,2,0:T(8,128)(2,1)S(1)} all-to-all(bf16[16,128,448]{1,2,0:T(8,128)(2,1)S(1)} %copy.37), channel_id=1, replica_groups=mesh['rep_0'=8,'rep_1'=2,'rep_2'=2,'fsdp'=16] {'rep_0','rep_1'}, dimensions={0} | all-to-all | bytes 3670016 | tf_op jit(solution)/shard_map/all_to_all | solution.py:50
  267.5 47.7 %all_to_all.44 = bf16[16,128,448]{1,2,0:T(8,128)(2,1)S(1)} all-to-all(bf16[16,128,448]{1,2,0:T(8,128)(2,1)S(1)} %broadcast_in_dim.12), channel_id=1, replica_groups=mesh['rep_0'=8,'rep_1'=2,'rep_2'=2,'fsdp'=16] {'rep_0','rep_1'}, dimensions={0} | all-to-all | bytes 3670016 | tf_op jit(solution)/shard_map/all_to_all | solution.py:12
  316.9 8.8 %all_to_all.45 = bf16[2,16,128,448]{2,1,3,0:T(8,128)(2,1)S(1)} all-to-all(bf16[2,16,128,448]{2,1,3,0:T(8,128)(2,1)S(1)} %broadcast_in_dim.13), channel_id=1, replica_groups=mesh['rep_0'=8,'rep_1'=2,'rep_2'=2,'fsdp'=16] {'rep_2'}, dimensions={0} | all-to-all | bytes 7340032 | tf_op jit(solution)/shard_map/all_to_all | solution.py:12
  325.6 7.5 %copy.39 = bf16[16,2,128,448]{2,1,0,3:T(2,128)(2,1)} copy(bf16[16,2,128,448]{2,0,3,1:T(8,128)(2,1)S(1)} %bitcast.34) | data formatting | bytes 7340032 | tf_op jit(solution)/shard_map/transpose | solution.py:26
  333.2 7.2 %reshape_reshape.11 = bf16[4096,448]{0,1:T(8,128)(2,1)} reshape(bf16[16,2,128,448]{2,1,0,3:T(2,128)(2,1)} %copy.39) | data formatting | bytes 7340032 | tf_op jit(solution)/shard_map/reshape;reshape | solution.py:20
  340.4 6.0 %fusion.9 = (f32[448]{0:T(512)S(1)}, f32[512,448]{0,1:T(8,128)S(1)}) fusion(f32[512,448]{0,1:T(8,128)S(1)} %copy-done.5, bf16[512,448]{0,1:T(8,128)(2,1)S(1)} %copy-done.2, bf16[512,448]{0,1:T(8,128)(2,1)S(1)} %copy-done.3, bf16[4096,448]{0,1:T(8,128)(2,1)} %reshape_reshape.11, bf16[512,4096]{0,1:T(8,128)(2,1)} %bitcast.1), kind=kOutput, calls=%fused_computation.17 | convolution fusion | flops 1883176448 | bytes 10618624 | tf_op jit(solution)/shard_map/dot_general | solution.py:101
  346.4 4.8 %fusion.2 = f32[448]{0:T(512)S(1)} fusion(f32[512,448]{0,1:T(8,128)S(1)} %get-tuple-element.6, bf16[448,4096]{1,0:T(8,128)(2,1)S(1)} %copy-done, bf16[512,4096]{0,1:T(8,128)(2,1)} %bitcast.1, f32[512,448]{0,1:T(8,128)S(1)} %copy-done.5, bf16[512,448]{0,1:T(8,128)(2,1)S(1)} %copy-done.2, bf16[512,448]{0,1:T(8,128)(2,1)S(1)} %copy-done.3), kind=kOutput, calls=%fused_computation.10 | convolution fusion | flops 1883176448 | bytes 10618624 | tf_op jit(solution)/shard_map/dot_general | solution.py:93
  352.0 3.9 %all-to-all-start.7 = ((f32[32,1,896]{2,1,0:T(1,128)}), f32[32,1,896]{2,1,0:T(1,128)S(1)}, u32[]{:S(2)}, u32[]{:S(2)}) async-start(f32[32,1,896]{2,1,0:T(1,128)} %broadcast_in_dim.14), calls=%async_computation.7 | async-start | bytes 229376 | tf_op jit(solution)/shard_map/all_to_all | solution.py:12
  357.4 7.6 %all-to-all-done.7 = f32[32,1,896]{2,1,0:T(1,128)S(1)} async-done(((f32[32,1,896]{2,1,0:T(1,128)}), f32[32,1,896]{2,1,0:T(1,128)S(1)}, u32[]{:S(2)}, u32[]{:S(2)}) %all-to-all-start.7) | async-done | bytes 114720 | tf_op jit(solution)/shard_map/all_to_all | solution.py:12
  (25 shorter events, 7.6 us)
Async XLA Ops:
  0.6 12.1 %copy-start.1 = (bf16[512,256]{1,0:T(8,128)(2,1)S(1)}, bf16[512,256]{1,0:T(8,128)(2,1)}, u32[]{:S(2)}) copy-start(bf16[512,256]{1,0:T(8,128)(2,1)} %param.4) | copy-start | bytes 786436
  3.2 51.5 %all-to-all-start.1 = ((bf16[16,128,448]{1,2,0:T(8,128)(2,1)}), bf16[16,128,448]{1,2,0:T(8,128)(2,1)S(1)}, u32[]{:S(2)}, u32[]{:S(2)}) async-start(bf16[16,128,448]{1,2,0:T(8,128)(2,1)} %broadcast_in_dim.10), calls=%async_computation.1 | async-start | bytes 3670016 | tf_op jit(solution)/shard_map/all_to_all | solution.py:12
  70.2 111.4 %all-to-all-start = ((bf16[16,512,256]{1,2,0:T(8,128)(2,1)}), bf16[16,512,256]{1,2,0:T(8,128)(2,1)}, u32[]{:S(2)}, u32[]{:S(2)}) async-start(bf16[16,512,256]{1,2,0:T(8,128)(2,1)} %stack.2), calls=%async_computation | async-start | bytes 8388608 | tf_op jit(solution)/shard_map/all_to_all | solution.py:77
  181.6 5.4 %copy-start.2 = (bf16[512,448]{0,1:T(8,128)(2,1)S(1)}, bf16[512,448]{0,1:T(8,128)(2,1)}, u32[]{:S(2)}) copy-start(bf16[512,448]{0,1:T(8,128)(2,1)} %param.6) | copy-start | bytes 1376260
  181.6 5.4 %copy-start.3 = (bf16[512,448]{0,1:T(8,128)(2,1)S(1)}, bf16[512,448]{0,1:T(8,128)(2,1)}, u32[]{:S(2)}) copy-start(bf16[512,448]{0,1:T(8,128)(2,1)} %param.7) | copy-start | bytes 1376260
  187.1 6.7 %copy-start.4 = (f32[512,448]{0,1:T(8,128)}, f32[512,448]{0,1:T(8,128)S(1)}, u32[]{:S(2)}) copy-start(f32[512,448]{0,1:T(8,128)S(1)} %fusion.13) | copy-start | bytes 2752516
  333.2 7.2 %copy-start.5 = (f32[512,448]{0,1:T(8,128)S(1)}, f32[512,448]{0,1:T(8,128)}, u32[]{:S(2)}) copy-start(f32[512,448]{0,1:T(8,128)} %copy-done.4) | copy-start | bytes 2752516
  340.4 6.0 %copy-start = (bf16[448,4096]{1,0:T(8,128)(2,1)S(1)}, bf16[448,4096]{1,0:T(8,128)(2,1)}, u32[]{:S(2)}) copy-start(bf16[448,4096]{1,0:T(8,128)(2,1)} %convolution_convert_fusion) | copy-start | bytes 11010052
  352.0 13.1 %all-to-all-start.7 = ((f32[32,1,896]{2,1,0:T(1,128)}), f32[32,1,896]{2,1,0:T(1,128)S(1)}, u32[]{:S(2)}, u32[]{:S(2)}) async-start(f32[32,1,896]{2,1,0:T(1,128)} %broadcast_in_dim.14), calls=%async_computation.7 | async-start | bytes 229376 | tf_op jit(solution)/shard_map/all_to_all | solution.py:12
